TPU v7x, 1024 devices: a whole 8x8x8 slice. The times are simulated.
1024 devices in a mesh: blk: 32 (over z, x_hi), inner: 32 (over y, x_lo, core).
Axes of the slice: x: 8 (x_hi: 4, x_lo: 2; x = x_hi * 2 + x_lo), y: 8, z: 8, core: 2. Of those that a mesh axis runs over, the one named last changes fastest.
Arguments:
- image_student: bfloat16 [229376, 1152], P(('blk', 'inner')), may hold values from -6 to 6
- text_student: bfloat16 [229376, 1152], P(('blk', 'inner')), may hold values from -6 to 6
- image_teacher: bfloat16 [229376, 1152], P(('blk', 'inner')), may hold values from -6 to 6
- text_teacher: bfloat16 [229376, 1152], P(('blk', 'inner')), may hold values from -6 to 6
- pair_ids: int32 [229376], replicated, may hold values from 0 to 28671
Outputs:
- image_grad: bfloat16 [229376, 1152], P(('blk', 'inner'))
- text_grad: bfloat16 [229376, 1152], P(('blk', 'inner'))
Inputs may be any that keep to these rules, and one draw needn't show every extreme that they name: Image row i and text row j form a positive pair exactly when pair_ids[i] == pair_ids[j]; every row is positive with its own text.
All inputs are finite; a program needn't handle non-finite values.
Results may differ from a plain program's by a relative error of at most 0.012.
Values may be sent and summed in bfloat16 or wider, within the bound.
A program may use at most 32 MiB of HBM per device.

v0:
```python
import functools

import jax
import jax.numpy as jnp
from jax import lax
from jax.experimental import pallas as pl
from jax.experimental.pallas import tpu as pltpu
from jax.sharding import PartitionSpec as P

MESH = pl.DeviceIdType.MESH
LANES = 128
PARTS = 2

logit_gain = 32.0
logit_shift = -2.0


def kernel(
    n_blk, n_inner, img_s, txt_s, img_t, txt_t, ids, image_grad, text_grad,
    IS, IT, TS, TT, XS, XT, SIG, SIGX, IDS, COL, H_OWN, H_ACC, H1S, H2S, H1R, H2R,
    G_OWN, GS, GR, GXS, GXR, G_OUT, H_OUT, RELAY,
    load_sem, img_sem, x_sem, p1_send, p1_recv, p2_send, p2_recv, fwd_send,
    h1_sem, h2_sem, g_sem, gx_sem, out_sem, relay_sem,
):
    rows, width = img_s.shape
    part = rows // PARTS
    gain = logit_gain / width
    n_dev = n_blk * n_inner
    blk, inner = lax.axis_index("blk"), lax.axis_index("inner")
    g = blk * n_inner + inner
    core = lax.rem(inner, 2)
    right_x = lax.rem(inner // 2, 2) == 1
    y = inner // 4
    top, bottom = y == n_inner // 4 - 1, y == 0
    c0, c1 = core == 0, core == 1
    no = jnp.logical_not

    has_p2 = c1 & no(bottom)
    forwards = has_p2 & right_x
    sends_p2 = c1 & no(top)
    first_one = g == 0
    wraps, wraps2 = g == n_dev - 2, g == n_dev - 3
    relays, relays2 = g == 3 * n_inner + 2, g == 4 * n_inner - 4
    sends_p1 = no(sends_p2 & right_x) & no(wraps)
    gets_h2 = sends_p2 | wraps2
    gets_x = c1 & ((right_x & top) | (no(right_x) & bottom)) & (g != n_dev - 1)
    sends_x = c0 & bottom & (g != 0)

    def block(shift):
        return lax.rem(g + shift + n_dev, n_dev)

    def at(shift):
        b = block(shift)
        return (b // n_inner, lax.rem(b, n_inner))

    def fixed(b):
        return (b // n_inner + 0 * blk, b % n_inner + 0 * inner)

    zero, relay, relay2 = fixed(0), fixed(3 * n_inner + 2), fixed(4 * n_inner - 4)
    mate = (blk, inner + 1 - 2 * core)
    after, before, after2, before2 = at(2), at(-2), at(4), at(jnp.where(first_one, -3, -4))
    step_up, step_down = at(1), at(-1)

    def piece(r):
        return pl.ds(r * part, part)

    def remote(src, dst, send, recv, to):
        return pltpu.make_async_remote_copy(
            src_ref=src, dst_ref=dst, send_sem=send, recv_sem=recv, device_id=to, device_id_type=MESH
        )

    loads = [
        pltpu.make_async_copy(src, dst, load_sem.at[i])
        for i, (src, dst) in enumerate(
            ((txt_s, TS.at[0]), (img_s, IS.at[0]), (txt_t, TT.at[0]), (img_t, IT.at[0]), (ids, IDS))
        )
    ]
    to_mate = [
        remote(src, dst, img_sem.at[0, i], img_sem.at[1, i], mate)
        for i, (src, dst) in enumerate(((img_s, IS.at[1]), (img_t, IT.at[1])))
    ]
    to_x = [
        remote(src, dst, x_sem.at[0, i], x_sem.at[1, i], step_down)
        for i, (src, dst) in enumerate(((img_s, XS), (img_t, XT)))
    ]
    p1, p2, fwd, to_relay, from_relay, to_relay2, from_relay2 = {}, {}, {}, {}, {}, {}, {}
    for r in range(PARTS):
        for i, (src, held) in enumerate(((txt_s, TS), (txt_t, TT))):
            k = 2 * r + i
            p1[r, i] = remote(src.at[piece(r)], held.at[1, piece(r)], p1_send.at[k], p1_recv.at[k], after)
            p2[r, i] = remote(src.at[piece(r)], held.at[2, piece(r)], p2_send.at[k], p2_recv.at[k], after2)
            to_relay[r, i] = remote(
                src.at[piece(r)], RELAY.at[i, piece(r)], relay_sem.at[0, k], relay_sem.at[1, k], relay
            )
            from_relay[r, i] = remote(
                RELAY.at[i, piece(r)], held.at[1, piece(r)], relay_sem.at[2, k], p1_recv.at[k], zero
            )
            to_relay2[r, i] = remote(
                src.at[piece(r)], RELAY.at[i, piece(r)], relay_sem.at[0, k], relay_sem.at[1, k], relay2
            )
            from_relay2[r, i] = remote(
                RELAY.at[i, piece(r)], held.at[2, piece(r)], relay_sem.at[2, k], p2_recv.at[k], zero
            )
            fwd[r, i] = remote(
                held.at[2, piece(r)], held.at[1, piece(r)], fwd_send.at[k], p1_recv.at[k], before
            )
    h1 = [remote(H1S.at[piece(r)], H1R.at[piece(r)], h1_sem.at[0, r], h1_sem.at[1, r], before) for r in range(PARTS)]
    h2 = [remote(H2S.at[piece(r)], H2R.at[piece(r)], h2_sem.at[0, r], h2_sem.at[1, r], before2) for r in range(PARTS)]
    g_copy = remote(GS, GR, g_sem.at[0], g_sem.at[1], mate)
    gx_copy = remote(GXS, GXR, gx_sem.at[0], gx_sem.at[1], step_up)
    g_out = pltpu.make_async_copy(G_OUT, image_grad, out_sem.at[PARTS])
    h_out = [
        pltpu.make_async_copy(H_OUT.at[piece(r)], text_grad.at[piece(r)], out_sem.at[r]) for r in range(PARTS)
    ]

    barrier = pltpu.get_barrier_semaphore()

    def greet(to):
        pl.semaphore_signal(barrier, inc=1, device_id=to, device_id_type=MESH)

    greet(mate)
    greet(before)

    @pl.when(has_p2)
    def _():
        greet(before2)

    @pl.when(has_p2 & no(right_x))
    def _():
        greet(after)

    @pl.when(gets_x)
    def _():
        greet(step_up)

    @pl.when(relays)
    def _():
        greet(fixed(n_dev - 2))

    @pl.when(relays2)
    def _():
        greet(fixed(n_dev - 3))

    @pl.when(first_one)
    def _():
        greet(relay2)

    for copy in loads:
        copy.start()
    peers = 2 + jnp.where(sends_p2, 1, 0) + jnp.where(forwards, 1, 0) + jnp.where(sends_x | wraps | wraps2 | relays2, 1, 0)
    pl.semaphore_wait(barrier, peers)

    @pl.when(sends_x)
    def _():
        for copy in to_x:
            copy.start()

    @pl.when(wraps)
    def _():
        for key in to_relay:
            to_relay[key].start()

    @pl.when(wraps2)
    def _():
        for key in to_relay2:
            to_relay2[key].start()

    @pl.when(sends_p1)
    def _():
        for key in p1:
            p1[key].start()

    @pl.when(sends_p2)
    def _():
        for key in p2:
            p2[key].start()

    for copy in to_mate:
        copy.start()

    for copy in loads:
        copy.wait()

    def lane_ids(b):
        start = b * rows
        first = jnp.minimum(start // LANES, IDS.shape[0] - 3)
        offset = start - first * LANES
        line = jnp.concatenate([IDS[pl.ds(first + i, 1), :] for i in range(3)], axis=1)
        line = jnp.broadcast_to(line.astype(jnp.float32), (8, 3 * LANES))
        return pltpu.roll(line, lax.rem(3 * LANES - offset, 3 * LANES), 1)[0:1]

    even = g - core
    own_ids = lane_ids(g)[:, :rows]
    mate_ids = lane_ids(even + 1 - core)[:, :rows]
    x_ids = lane_ids(block(1))[:, :rows]
    for q, b in enumerate((g, block(-2), block(jnp.where(first_one, -3, -4)))):
        COL[q] = jnp.transpose(jnp.broadcast_to(lane_ids(b)[:, : 2 * LANES], (LANES, 2 * LANES)))

    def nt(a, b):
        return lax.dot_general(a, b, (((1,), (1,)), ((), ())), preferred_element_type=jnp.float32)

    def tn(a, b):
        return lax.dot_general(a, b, (((0,), (0,)), ((), ())), preferred_element_type=jnp.float32)

    def nn(a, b):
        return jnp.dot(a, b, preferred_element_type=jnp.float32)

    def signal(q, r, student_img, teacher_img, img_ids):
        span = pl.ds(0, rows) if r is None else piece(r)
        student = (0.5 * gain) * nt(TS[q, span], student_img[...]) + 0.5 * logit_shift
        teacher = (0.5 * gain) * nt(TT[q, span], teacher_img[...]) + 0.5 * logit_shift
        same = jnp.where(COL[q, span, 0:1] == img_ids, 0.5, 0.0)
        target = same + (0.25 + 0.25 * jnp.tanh(teacher))
        return ((0.5 + 0.5 * jnp.tanh(student)) - target).astype(jnp.bfloat16)

    own = signal(0, None, IS.at[0], IT.at[0], own_ids)
    SIG[0, 0] = own
    H_OWN[...] = nn(own, IS[0])
    for copy in to_mate:
        copy.wait_recv()

    @pl.when(c0)
    def _():
        other = signal(0, None, IS.at[1], IT.at[1], mate_ids)
        SIG[0, 1] = other
        H_OWN[...] += nn(other, IS[1])

    def second(r, m, img_ids):
        for i in range(2):
            p2[r, i].wait_recv()

            @pl.when(forwards)
            def _():
                fwd[r, i].start()

        other = signal(2, r, IS.at[m], IT.at[m], img_ids)
        SIG[2, m, piece(r)] = other
        H2S[piece(r)] = nn(other, IS[m]).astype(jnp.bfloat16)
        h2[r].start()

    def first(r):
        for i in range(2):
            p1[r, i].wait_recv()
        near = signal(1, r, IS.at[0], IT.at[0], own_ids)
        SIG[1, 0, piece(r)] = near
        other = signal(1, r, IS.at[1], IT.at[1], mate_ids)
        SIG[1, 1, piece(r)] = other
        H_ACC[...] = nn(near, IS[0]) + nn(other, IS[1])

        @pl.when(gets_x)
        def _():
            if r == 0:
                for copy in to_x:
                    copy.wait_recv()
            far = signal(1, r, XS, XT, x_ids)
            SIGX[piece(r)] = far
            H_ACC[...] += nn(far, XS[...])

        H1S[piece(r)] = H_ACC[...].astype(jnp.bfloat16)
        h1[r].start()

    @pl.when(has_p2)
    def _():
        second(0, 1, mate_ids)

    @pl.when(has_p2 & right_x)
    def _():
        second(1, 1, mate_ids)

    first(0)

    @pl.when(has_p2 & no(right_x))
    def _():
        second(1, 1, mate_ids)

    @pl.when(relays)
    def _():
        for i in range(2):
            to_relay[0, i].wait_recv()
            from_relay[0, i].start()

    first(1)

    @pl.when(relays)
    def _():
        for i in range(2):
            to_relay[1, i].wait_recv()
            from_relay[1, i].start()

    @pl.when(relays2)
    def _():
        for key in to_relay2:
            to_relay2[key].wait_recv()
            from_relay2[key].start()

    @pl.when(gets_x)
    def _():
        GXS[...] = tn(SIGX[...], TS[1]).astype(jnp.bfloat16)
        gx_copy.start()

    G_OWN[...] = tn(SIG[1, 1], TS[1])

    @pl.when(c0)
    def _():
        G_OWN[...] += tn(SIG[0, 1], TS[0])

    @pl.when(has_p2)
    def _():
        G_OWN[...] += tn(SIG[2, 1], TS[2])

    GS[...] = G_OWN[...].astype(jnp.bfloat16)
    g_copy.start()
    G_OWN[...] = tn(SIG[0, 0], TS[0]) + tn(SIG[1, 0], TS[1])

    @pl.when(first_one)
    def _():
        second(0, 0, own_ids)
        second(1, 0, own_ids)
        G_OWN[...] += tn(SIG[2, 0], TS[2])

    @pl.when(sends_x)
    def _():
        gx_copy.wait_recv()
        G_OWN[...] += GXR[...].astype(jnp.float32)

    g_copy.wait_recv()
    G_OUT[...] = (gain * (G_OWN[...] + GR[...].astype(jnp.float32))).astype(jnp.bfloat16)
    g_out.start()

    for r in range(PARTS):
        @pl.when(gets_h2)
        def _():
            h2[r].wait_recv()
            H_OWN[piece(r)] += H2R[piece(r)].astype(jnp.float32)

        h1[r].wait_recv()
        H_OUT[piece(r)] = (gain * (H_OWN[piece(r)] + H1R[piece(r)].astype(jnp.float32))).astype(jnp.bfloat16)
        h_out[r].start()

    for copy in to_mate + h1 + [g_copy]:
        copy.wait_send()

    @pl.when(sends_p1)
    def _():
        for key in p1:
            p1[key].wait_send()

    @pl.when(wraps)
    def _():
        for key in to_relay:
            to_relay[key].wait_send()

    @pl.when(relays)
    def _():
        for key in from_relay:
            from_relay[key].wait_send()

    @pl.when(sends_p2)
    def _():
        for key in p2:
            p2[key].wait_send()

    @pl.when(forwards)
    def _():
        for key in fwd:
            fwd[key].wait_send()

    @pl.when(relays2)
    def _():
        for key in from_relay2:
            from_relay2[key].wait_send()

    @pl.when(wraps2)
    def _():
        for key in to_relay2:
            to_relay2[key].wait_send()

    @pl.when(has_p2 | first_one)
    def _():
        for copy in h2:
            copy.wait_send()

    @pl.when(sends_x)
    def _():
        for copy in to_x:
            copy.wait_send()

    @pl.when(gets_x)
    def _():
        gx_copy.wait_send()

    for copy in h_out + [g_out]:
        copy.wait()


def local(n_blk, n_inner, image_student, text_student, image_teacher, text_teacher, pair_ids):
    rows, width = image_student.shape
    bf, f32 = jnp.bfloat16, jnp.float32
    VM, DMA = pltpu.VMEM, pltpu.SemaphoreType.DMA
    ids = pair_ids.reshape(-1, LANES)
    part = rows // PARTS
    one = (rows, width)
    return pl.pallas_call(
        functools.partial(kernel, n_blk, n_inner),
        out_shape=(jax.ShapeDtypeStruct(one, bf), jax.ShapeDtypeStruct(one, bf)),
        in_specs=[pl.BlockSpec(memory_space=pl.ANY)] * 5,
        out_specs=(pl.BlockSpec(memory_space=pl.ANY),) * 2,
        scratch_shapes=[
            VM((2, *one), bf), VM((2, *one), bf),
            VM((3, *one), bf), VM((3, *one), bf),
            VM(one, bf), VM(one, bf),
            VM((3, 2, rows, rows), bf), VM((rows, rows), bf),
            VM(ids.shape, jnp.int32), VM((3, 2 * LANES, LANES), f32),
            VM(one, f32), VM((part, width), f32),
            VM(one, bf), VM(one, bf), VM(one, bf), VM(one, bf),
            VM(one, f32), VM(one, bf), VM(one, bf), VM(one, bf), VM(one, bf),
            VM(one, bf), VM(one, bf), VM((2, *one), bf),
            DMA((5,)), DMA((2, 2)), DMA((2, 2)),
            DMA((2 * PARTS,)), DMA((2 * PARTS,)), DMA((2 * PARTS,)), DMA((2 * PARTS,)), DMA((2 * PARTS,)),
            DMA((2, PARTS)), DMA((2, PARTS)), DMA((2,)), DMA((2,)), DMA((PARTS + 1,)), DMA((3, 2 * PARTS)),
        ],
        compiler_params=pltpu.CompilerParams(
            collective_id=0, has_side_effects=True, vmem_limit_bytes=60 << 20
        ),
        name="window_grads",
    )(image_student, text_student, image_teacher, text_teacher, ids)


def solution(mesh):
    both = P(("blk", "inner"), None)
    return jax.shard_map(
        functools.partial(local, mesh.shape["blk"], mesh.shape["inner"]),
        mesh=mesh,
        in_specs=(both, both, both, both, P()),
        out_specs=(both, both),
        check_vma=False,
    )
```

profile of v0, /device:TPU:1, one launch (start us, length us, event | category | flops | bytes accessed | tf_op | source)
XLA Modules:
  0.0 51.5 jit_solution(11611902327039860734)
XLA Ops:
  0.6 48.1 %window_grads.1 = (bf16[224,1152]{1,0:T(8,128)(2,1)}, bf16[224,1152]{1,0:T(8,128)(2,1)}) custom-call(bf16[224,1152]{1,0:T(8,128)(2,1)} %img_s.1, bf16[224,1152]{1,0:T(8,128)(2,1)} %txt_s.1, bf16[224,1152]{1,0:T(8,128)(2,1)} %img_t.1, bf16[224,1152]{1,0:T(8,128)(2,1)} %txt_t.1, s32[1792,128]{1,0:T(8,128)} %bitcast.1), custom_call_target="tpu_custom_call" | custom-call | tf_op jit(solution)/shard_map/window_grads/pallas_call | solution.py:403
  48.8 0.0 copy-start
  48.8 1.9 %copy.9 = bf16[224,1152]{1,0:T(8,128)(2,1)} copy(bf16[224,1152]{1,0:T(8,128)(2,1)} %get-tuple-element.4) | data formatting | bytes 1032192
  50.7 0.0 copy-done
  50.7 0.8 %copy.10 = bf16[224,1152]{1,0:T(8,128)(2,1)} copy(bf16[224,1152]{1,0:T(8,128)(2,1)S(1)} %copy-done) | data formatting | bytes 1032192
Async XLA Ops:
  48.8 1.9 %copy-start = (bf16[224,1152]{1,0:T(8,128)(2,1)S(1)}, bf16[224,1152]{1,0:T(8,128)(2,1)}, u32[]{:S(2)}) copy-start(bf16[224,1152]{1,0:T(8,128)(2,1)} %get-tuple-element.5) | copy-start | bytes 1548292
where the time goes:
time: 51.7 us; the launch traced here: 51.5 us
  Pallas kernels  48.1 us (93%)
  local copies, waits for them, and re-layouts  2.71 us (5%)
  between operations  0.65 us (1%)
    pallas_call x1, Pallas kernels, local(): pl.pallas_call(functools.partial(kernel, n_blk, n_inner), out_shape=(jax....  48.1 us
    unnamed x4, local copies, waits for them, and re-layouts  2.71 us

commit v1 on v0

--- a/solution.py
+++ b/solution.py
@@ -20,7 +20,7 @@
     IS, IT, TS, TT, XS, XT, SIG, SIGX, IDS, COL, H_OWN, H_ACC, H1S, H2S, H1R, H2R,
     G_OWN, GS, GR, GXS, GXR, G_OUT, H_OUT, RELAY,
     load_sem, img_sem, x_sem, p1_send, p1_recv, p2_send, p2_recv, fwd_send,
-    h1_sem, h2_sem, g_sem, gx_sem, out_sem, relay_sem,
+    h1_sem, h2_sem, g_sem, gx_sem, out_sem, relay_sem, back_sem, go_sem,
 ):
     rows, width = img_s.shape
     part = rows // PARTS
@@ -38,13 +38,13 @@
     has_p2 = c1 & no(bottom)
     forwards = has_p2 & right_x
     sends_p2 = c1 & no(top)
-    first_one = g == 0
-    wraps, wraps2 = g == n_dev - 2, g == n_dev - 3
-    relays, relays2 = g == 3 * n_inner + 2, g == 4 * n_inner - 4
+    first_two, second_even = (g == 0) | (g == 2), g == 2
+    passes = (g == 1) | (g == n_dev - 1)
+    wraps, relays = g == n_dev - 2, g == 3 * n_inner + 2
     sends_p1 = no(sends_p2 & right_x) & no(wraps)
-    gets_h2 = sends_p2 | wraps2
-    gets_x = c1 & ((right_x & top) | (no(right_x) & bottom)) & (g != n_dev - 1)
-    sends_x = c0 & bottom & (g != 0)
+    gets_h2 = sends_p2 | (g == n_dev - 3) | (g == n_dev - 1)
+    gets_x = c1 & ((right_x & top) | (no(right_x) & bottom)) & no(passes)
+    sends_x = c0 & bottom & no(first_two)
 
     def block(shift):
         return lax.rem(g + shift + n_dev, n_dev)
@@ -56,9 +56,9 @@
     def fixed(b):
         return (b // n_inner + 0 * blk, b % n_inner + 0 * inner)
 
-    zero, relay, relay2 = fixed(0), fixed(3 * n_inner + 2), fixed(4 * n_inner - 4)
+    zero, relay = fixed(0), fixed(3 * n_inner + 2)
     mate = (blk, inner + 1 - 2 * core)
-    after, before, after2, before2 = at(2), at(-2), at(4), at(jnp.where(first_one, -3, -4))
+    after, before, after2, before2 = at(2), at(-2), at(4), at(jnp.where(first_two, -3, -4))
     step_up, step_down = at(1), at(-1)
 
     def piece(r):
@@ -83,7 +83,7 @@
         remote(src, dst, x_sem.at[0, i], x_sem.at[1, i], step_down)
         for i, (src, dst) in enumerate(((img_s, XS), (img_t, XT)))
     ]
-    p1, p2, fwd, to_relay, from_relay, to_relay2, from_relay2 = {}, {}, {}, {}, {}, {}, {}
+    p1, p2, fwd, to_relay, from_relay, ahead = {}, {}, {}, {}, {}, {}
     for r in range(PARTS):
         for i, (src, held) in enumerate(((txt_s, TS), (txt_t, TT))):
             k = 2 * r + i
@@ -95,17 +95,18 @@
             from_relay[r, i] = remote(
                 RELAY.at[i, piece(r)], held.at[1, piece(r)], relay_sem.at[2, k], p1_recv.at[k], zero
             )
-            to_relay2[r, i] = remote(
-                src.at[piece(r)], RELAY.at[i, piece(r)], relay_sem.at[0, k], relay_sem.at[1, k], relay2
-            )
-            from_relay2[r, i] = remote(
-                RELAY.at[i, piece(r)], held.at[2, piece(r)], relay_sem.at[2, k], p2_recv.at[k], zero
+            ahead[r, i] = remote(
+                held.at[1, piece(r)], held.at[2, piece(r)], relay_sem.at[2, k], p2_recv.at[k], step_up
             )
             fwd[r, i] = remote(
                 held.at[2, piece(r)], held.at[1, piece(r)], fwd_send.at[k], p1_recv.at[k], before
             )
     h1 = [remote(H1S.at[piece(r)], H1R.at[piece(r)], h1_sem.at[0, r], h1_sem.at[1, r], before) for r in range(PARTS)]
     h2 = [remote(H2S.at[piece(r)], H2R.at[piece(r)], h2_sem.at[0, r], h2_sem.at[1, r], before2) for r in range(PARTS)]
+    back = [
+        remote(H2S.at[piece(r)], GXR.at[piece(r)], back_sem.at[0, r], back_sem.at[1, r], before) for r in range(PARTS)
+    ]
+    on = [remote(GXR.at[piece(r)], H2R.at[piece(r)], back_sem.at[2, r], h2_sem.at[1, r], step_down) for r in range(PARTS)]
     g_copy = remote(GS, GR, g_sem.at[0], g_sem.at[1], mate)
     gx_copy = remote(GXS, GXR, gx_sem.at[0], gx_sem.at[1], step_up)
     g_out = pltpu.make_async_copy(G_OUT, image_grad, out_sem.at[PARTS])
@@ -118,9 +119,12 @@
     def greet(to):
         pl.semaphore_signal(barrier, inc=1, device_id=to, device_id_type=MESH)
 
-    greet(mate)
     greet(before)
 
+    @pl.when(c1)
+    def _():
+        greet(mate)
+
     @pl.when(has_p2)
     def _():
         greet(before2)
@@ -137,17 +141,13 @@
     def _():
         greet(fixed(n_dev - 2))
 
-    @pl.when(relays2)
-    def _():
-        greet(fixed(n_dev - 3))
-
-    @pl.when(first_one)
-    def _():
-        greet(relay2)
+    @pl.when(first_two)
+    def _():
+        greet(step_down)
 
     for copy in loads:
         copy.start()
-    peers = 2 + jnp.where(sends_p2, 1, 0) + jnp.where(forwards, 1, 0) + jnp.where(sends_x | wraps | wraps2 | relays2, 1, 0)
+    peers = 2 - core + jnp.where(sends_p2, 1, 0) + jnp.where(forwards, 1, 0) + jnp.where(sends_x | wraps | passes, 1, 0)
     pl.semaphore_wait(barrier, peers)
 
     @pl.when(sends_x)
@@ -160,23 +160,24 @@
         for key in to_relay:
             to_relay[key].start()
 
-    @pl.when(wraps2)
-    def _():
-        for key in to_relay2:
-            to_relay2[key].start()
-
-    @pl.when(sends_p1)
+    @pl.when(sends_p1 & no(second_even))
     def _():
         for key in p1:
             p1[key].start()
 
+    @pl.when(g == 0)
+    def _():
+        pl.semaphore_signal(go_sem, inc=1, device_id=after, device_id_type=MESH)
+
     @pl.when(sends_p2)
     def _():
         for key in p2:
             p2[key].start()
 
-    for copy in to_mate:
-        copy.start()
+    @pl.when(c0)
+    def _():
+        for copy in to_mate:
+            copy.start()
 
     for copy in loads:
         copy.wait()
@@ -193,7 +194,7 @@
     own_ids = lane_ids(g)[:, :rows]
     mate_ids = lane_ids(even + 1 - core)[:, :rows]
     x_ids = lane_ids(block(1))[:, :rows]
-    for q, b in enumerate((g, block(-2), block(jnp.where(first_one, -3, -4)))):
+    for q, b in enumerate((g, block(-2), block(jnp.where(first_two, -3, -4)))):
         COL[q] = jnp.transpose(jnp.broadcast_to(lane_ids(b)[:, : 2 * LANES], (LANES, 2 * LANES)))
 
     def nt(a, b):
@@ -219,12 +220,23 @@
     for copy in to_mate:
         copy.wait_recv()
 
+    @pl.when(c1)
+    def _():
+        for copy in to_mate:
+            copy.start()
+
     @pl.when(c0)
     def _():
         other = signal(0, None, IS.at[1], IT.at[1], mate_ids)
         SIG[0, 1] = other
         H_OWN[...] += nn(other, IS[1])
 
+    @pl.when(second_even)
+    def _():
+        pl.semaphore_wait(go_sem, 1)
+        for key in p1:
+            p1[key].start()
+
     def second(r, m, img_ids):
         for i in range(2):
             p2[r, i].wait_recv()
@@ -236,11 +248,23 @@
         other = signal(2, r, IS.at[m], IT.at[m], img_ids)
         SIG[2, m, piece(r)] = other
         H2S[piece(r)] = nn(other, IS[m]).astype(jnp.bfloat16)
-        h2[r].start()
+
+        @pl.when(second_even)
+        def _():
+            back[r].start()
+
+        @pl.when(no(second_even))
+        def _():
+            h2[r].start()
 
     def first(r):
         for i in range(2):
             p1[r, i].wait_recv()
+
+            @pl.when(passes)
+            def _():
+                ahead[r, i].start()
+
         near = signal(1, r, IS.at[0], IT.at[0], own_ids)
         SIG[1, 0, piece(r)] = near
         other = signal(1, r, IS.at[1], IT.at[1], mate_ids)
@@ -287,12 +311,6 @@
             to_relay[1, i].wait_recv()
             from_relay[1, i].start()
 
-    @pl.when(relays2)
-    def _():
-        for key in to_relay2:
-            to_relay2[key].wait_recv()
-            from_relay2[key].start()
-
     @pl.when(gets_x)
     def _():
         GXS[...] = tn(SIGX[...], TS[1]).astype(jnp.bfloat16)
@@ -312,7 +330,13 @@
     g_copy.start()
     G_OWN[...] = tn(SIG[0, 0], TS[0]) + tn(SIG[1, 0], TS[1])
 
-    @pl.when(first_one)
+    @pl.when(g == 0)
+    def _():
+        for r in range(PARTS):
+            back[r].wait_recv()
+            on[r].start()
+
+    @pl.when(first_two)
     def _():
         second(0, 0, own_ids)
         second(1, 0, own_ids)
@@ -365,19 +389,24 @@
         for key in fwd:
             fwd[key].wait_send()
 
-    @pl.when(relays2)
-    def _():
-        for key in from_relay2:
-            from_relay2[key].wait_send()
-
-    @pl.when(wraps2)
-    def _():
-        for key in to_relay2:
-            to_relay2[key].wait_send()
-
-    @pl.when(has_p2 | first_one)
+    @pl.when(passes)
+    def _():
+        for key in ahead:
+            ahead[key].wait_send()
+
+    @pl.when(has_p2 | (g == 0))
     def _():
         for copy in h2:
+            copy.wait_send()
+
+    @pl.when(second_even)
+    def _():
+        for copy in back:
+            copy.wait_send()
+
+    @pl.when(g == 0)
+    def _():
+        for copy in on:
             copy.wait_send()
 
     @pl.when(sends_x)
@@ -417,13 +446,13 @@
             VM(one, bf), VM(one, bf), VM((2, *one), bf),
             DMA((5,)), DMA((2, 2)), DMA((2, 2)),
             DMA((2 * PARTS,)), DMA((2 * PARTS,)), DMA((2 * PARTS,)), DMA((2 * PARTS,)), DMA((2 * PARTS,)),
-            DMA((2, PARTS)), DMA((2, PARTS)), DMA((2,)), DMA((2,)), DMA((PARTS + 1,)), DMA((3, 2 * PARTS)),
+            DMA((2, PARTS)), DMA((2, PARTS)), DMA((2,)), DMA((2,)), DMA((PARTS + 1,)), DMA((3, 2 * PARTS)), DMA((3, PARTS)), pltpu.SemaphoreType.REGULAR,
         ],
         compiler_params=pltpu.CompilerParams(
-            collective_id=0, has_side_effects=True, vmem_limit_bytes=60 << 20
+            collective_id=0, has_side_effects=True, vmem_limit_bytes=48 << 20
         ),
         name="window_grads",
-    )(image_student, text_student, image_teacher, text_teacher, ids)
+    )(*[pltpu.with_memory_space_constraint(a, pltpu.HBM) for a in (image_student, text_student, image_teacher, text_teacher, ids)])
 
 
 def solution(mesh):

time: 51.7 us -> 49.4 us (0.956)
  local copies, waits for them, and re-layouts: 2.71 us -> 1.57 us
  Pallas kernels: 48.1 us -> 47 us
    unnamed x4 -> x2, local copies, waits for them, and re-layouts: 2.71 us -> 1.57 us
    pallas_call x1, Pallas kernels: 48.1 us -> 47 us  [local(): pl.pallas_call(functools.partial(kernel, n_blk, n_inner), out_shape=(jax....]
where the time goes in v1:
time: 49.4 us; the launch traced here: 49.2 us
  Pallas kernels  47 us (95%)
  local copies, waits for them, and re-layouts  1.57 us (3%)
  between operations  0.64 us (1%)
    pallas_call x1, Pallas kernels, local(): pl.pallas_call(functools.partial(kernel, n_blk, n_inner), out_shape=(jax....  47 us
    unnamed x2, local copies, waits for them, and re-layouts  1.57 us

profile of v1, /device:TPU:1, one launch (start us, length us, event | category | flops | bytes accessed | tf_op | source)
XLA Modules:
  0.0 49.2 jit_solution(7833017563526713044)
XLA Ops:
  0.6 47.0 %window_grads.1 = (bf16[224,1152]{1,0:T(8,128)(2,1)S(1)}, bf16[224,1152]{1,0:T(8,128)(2,1)S(1)}) custom-call(bf16[224,1152]{1,0:T(8,128)(2,1)} %img_s.1, bf16[224,1152]{1,0:T(8,128)(2,1)} %txt_s.1, bf16[224,1152]{1,0:T(8,128)(2,1)} %img_t.1, bf16[224,1152]{1,0:T(8,128)(2,1)} %txt_t.1, s32[1792,128]{1,0:T(8,128)} %bitcast.1), custom_call_target="tpu_custom_call" | custom-call | tf_op jit(solution)/shard_map/window_grads/pallas_call | solution.py:432
  47.6 0.8 %copy.9 = bf16[224,1152]{1,0:T(8,128)(2,1)} copy(bf16[224,1152]{1,0:T(8,128)(2,1)S(1)} %get-tuple-element.4) | data formatting | bytes 1032192
  48.4 0.8 %copy.10 = bf16[224,1152]{1,0:T(8,128)(2,1)} copy(bf16[224,1152]{1,0:T(8,128)(2,1)S(1)} %get-tuple-element.5) | data formatting | bytes 1032192
